TPU v7x, 512 devices: a whole 4x8x8 slice. The times are simulated.
512 devices in a mesh: src: 8 (over x, y_lo), gx: 16 (over z, core), gy: 4 (over y_hi).
Axes of the slice: x: 4, y: 8 (y_hi: 4, y_lo: 2; y = y_hi * 2 + y_lo), z: 8, core: 2. Of those that a mesh axis runs over, the one named last changes fastest.
Arguments:
- warm_potential: float32 [32, 64, 128, 128], P('src', 'gx', 'gy'), may hold values from -3 to 3
- warm_adjoint: float32 [32, 64, 128, 128], P('src', 'gx', 'gy'), may hold values from -3 to 3
- conductivity: float32 [64, 128, 128], P('gx', 'gy', 'src'), may hold values from 0.2 to 5
- electrodes: int32 [32, 2], replicated, may hold values from 0 to 8191
- receivers: int32 [128, 2], replicated, may hold values from 0 to 8191
- observed: float32 [32, 128], replicated, may hold values from -6 to 6
- source_order: int32 [32], replicated, may hold values from 0 to 31, each once
Outputs:
- gradient: float32 [64, 128, 128], P('gx', 'gy', 'src')
Inputs may be any that keep to these rules, and one draw needn't show every extreme that they name: `electrodes`: entries number surface cells as x * 128 + y. `receivers`: entries number surface cells as x * 128 + y.
All inputs are finite; a program needn't handle non-finite values.
Results may differ from a plain program's by a relative error of at most 0.0003.
Values sent between devices are 32-bit elements; how exact they have to be, the bound alone decides.
A program may use at most 64 MiB of HBM per device.

v0:
```python
import jax
import jax.numpy as jnp
from jax import lax
from jax.sharding import PartitionSpec as P

SWEEPS = 6
lowest = 0.05
highest = 2.0
centre = (highest + lowest) / 2.0
half_span = (highest - lowest) / 2.0
bound_ratio = centre / half_span
strength = 4.0


def padded_2(block, sides, width):
    for axis, dim in sides:
        count = lax.axis_size(axis)
        forward = [(i, i + 1) for i in range(count - 1)]
        backward = [(target, source) for source, target in forward]
        low = lax.ppermute(
            lax.slice_in_dim(block, block.shape[dim] - width, None, axis=dim), axis, forward
        )
        high = lax.ppermute(lax.slice_in_dim(block, 0, width, axis=dim), axis, backward)
        block = jnp.concatenate([low, block, high], axis=dim)
    return block


def harmonic(left, right):
    return jnp.where(right > 0, 2.0 * left * right / (left + right), left)


def slope_of(left, right):
    total = left + right
    return jnp.where(right > 0, 2.0 * right * right / (total * total), 1.0)


def neighbours(field, padded):
    widths = [(0, 0)] * (field.ndim - 1) + [(1, 1)]
    deeper = jnp.pad(field, widths)
    return (
        padded[..., :-2, 1:-1, :],
        padded[..., 2:, 1:-1, :],
        padded[..., 1:-1, :-2, :],
        padded[..., 1:-1, 2:, :],
        deeper[..., :-2],
        deeper[..., 2:],
    )


def face_tables(sigma, padded):
    others = neighbours(sigma, padded)
    depth = lax.broadcasted_iota(jnp.int32, sigma.shape, 2)
    surface = depth == 0
    coeffs = [harmonic(sigma, other) for other in others]
    slopes = [slope_of(sigma, other) for other in others]
    coeffs[4] = jnp.where(surface, 0.0, coeffs[4])
    slopes[4] = jnp.where(surface, 0.0, slopes[4])
    return (coeffs, slopes)


def apply_operator(field, padded, coeffs):
    others = neighbours(field, padded)
    total = coeffs[0] * (field - others[0])
    for index in range(1, 6):
        total = total + coeffs[index] * (field - others[index])
    return total


def solve(rhs, start, coeffs, inverse, pad_fn):
    residual = rhs - apply_operator(start, pad_fn(start), coeffs)
    update = inverse * residual / centre
    iterate = start
    factor = 1.0 / bound_ratio
    for sweep in range(SWEEPS):
        iterate = iterate + update
        residual = residual - apply_operator(update, pad_fn(update), coeffs)
        following = 1.0 / (2.0 * bound_ratio - factor)
        update = following * factor * update + 2.0 * following / half_span * (inverse * residual)
        factor = following
    return iterate + update


def gradient_term(potential, adjoint, padded_potential, padded_adjoint, slopes):
    near_potential = neighbours(potential, padded_potential)
    near_adjoint = neighbours(adjoint, padded_adjoint)
    total = slopes[0] * (potential - near_potential[0]) * (adjoint - near_adjoint[0])
    for index in range(1, 6):
        total = total + slopes[index] * (potential - near_potential[index]) * (
            adjoint - near_adjoint[index]
        )
    return total


def pad_joint(field):
    return padded_2(field, (("gx", 1), ("gy", 2)), 1)


def reduce_groups(partial_value, depth):
    summed = lax.psum(partial_value, "src")
    return lax.dynamic_slice_in_dim(summed, lax.axis_index("src") * depth, depth, 2)


def body(warm_potential, warm_adjoint, conductivity, electrodes, receivers, observed, source_order):
    panel = lax.all_gather(conductivity, "src", axis=2, tiled=True)
    group = lax.axis_index("src")
    slots = warm_potential.shape[0]
    width_x = panel.shape[0]
    ny_global = panel.shape[1] * lax.axis_size("gy")
    x_start = lax.axis_index("gx") * width_x
    potential_start, adjoint_start = (warm_potential, warm_adjoint)
    first_slot = group * slots
    y_start = lax.axis_index("gy") * panel.shape[1]
    width_y = panel.shape[1]
    depth_cells = panel.shape[2]
    coeffs, slopes = face_tables(panel, pad_joint(panel[None])[0])
    inverse = 1.0 / (coeffs[0] + coeffs[1] + coeffs[2] + coeffs[3] + coeffs[4] + coeffs[5])
    idents = lax.dynamic_slice_in_dim(source_order, first_slot, slots)
    pairs = jnp.take(electrodes, idents, axis=0)
    rows_observed = jnp.take(observed, idents, axis=0)

    def picker(cells):
        local_x = cells // ny_global - x_start
        local_y = cells % ny_global - y_start
        inside = (local_x >= 0) & (local_x < width_x) & (local_y >= 0) & (local_y < width_y)
        flat = local_x * width_y + local_y
        places = lax.broadcasted_iota(jnp.int32, (cells.shape[0], width_x * width_y), 1)
        return jnp.where((flat[:, None] == places) & inside[:, None], 1.0, 0.0).astype(jnp.float32)

    def on_surface(flat):
        field = jnp.zeros((slots, width_x, width_y, depth_cells), jnp.float32)
        return field.at[..., 0].set(flat.reshape(slots, width_x, width_y))

    source_surface = strength * (picker(pairs[:, 0]) - picker(pairs[:, 1]))
    potential = solve(on_surface(source_surface), potential_start, coeffs, inverse, pad_joint)
    pickup = picker(receivers[:, 0]) - picker(receivers[:, 1])
    top = potential[..., 0].reshape(slots, width_x * width_y)
    local_values = jnp.dot(
        top, pickup.T, precision=lax.Precision.HIGHEST, preferred_element_type=jnp.float32
    )
    predicted = lax.psum(local_values, ("gx", "gy"))
    misfit = predicted - rows_observed
    back = jnp.dot(
        misfit, pickup, precision=lax.Precision.HIGHEST, preferred_element_type=jnp.float32
    )
    adjoint = solve(on_surface(back), adjoint_start, coeffs, inverse, pad_joint)
    padded_both = pad_joint(jnp.concatenate([potential, adjoint], 0))
    term = gradient_term(potential, adjoint, padded_both[:slots], padded_both[slots:], slopes)
    partial_value = -jnp.sum(term, axis=0)
    return reduce_groups(partial_value, conductivity.shape[2])


def solution(mesh):
    in_specs = (
        P("src", "gx", "gy", None),
        P("src", "gx", "gy", None),
        P("gx", "gy", "src"),
        P(),
        P(),
        P(),
        P(),
    )
    out_specs = P("gx", "gy", "src")
    return jax.shard_map(body, mesh=mesh, in_specs=in_specs, out_specs=out_specs, check_vma=False)
```

profile of v0, /device:TPU:16, one launch (start us, length us, event | category | flops | bytes accessed | tf_op | source)
XLA Modules:
  0.0 592.4 jit_solution(16727907163246744626)
XLA Ops:
  7.3 29.0 %all_gather.3 = f32[4,32,128]{1,0,2:T(4,128)S(1)} all-gather(f32[4,32,16]{1,0,2:T(4,128)S(1)} %copy.69), channel_id=1, replica_groups=mesh['src'=8,'gx'=16,'gy'=4] {'src'}, dimensions={2}, use_global_device_ids=true | all-gather | bytes 73728 | tf_op jit(solution)/shard_map/all_gather | solution.py:104
  58.0 21.9 %collective-permute-done.3 = f32[1,6,1,128]{2,1,3,0:T(8,128)S(1)} collective-permute-done((f32[1,6,1,128]{2,1,3,0:T(8,128)S(1)}, f32[1,6,1,128]{2,1,3,0:T(8,128)S(1)}, u32[]{:S(2)}, u32[]{:S(2)}) %collective-permute-start.3) | collective-permute-done | bytes 3104 | tf_op jit(solution)/shard_map/ppermute | solution.py:23
  84.7 5.6 collective-permute-start.6
  102.4 6.0 %collective-permute-start.10 = (f32[4,6,1,128]{3,2,1,0:T(1,128)S(1)}, f32[4,6,1,128]{3,2,1,0:T(1,128)S(1)}, u32[]{:S(2)}, u32[]{:S(2)}) collective-permute-start(f32[4,6,1,128]{3,2,1,0:T(1,128)S(1)} %get-tuple-element.118), channel_id=1, source_target_pairs={{0,1},{1,2},{2,3},{4,5},{5,6},{6,7},{8,9},{9,10},{10,11},{12,13},{... | collective-permute-start | bytes 36872 | tf_op jit(solution)/shard_map/ppermute | solution.py:20
  111.4 5.8 collective-permute-start.12
  120.1 6.0 %collective-permute-start.14 = (f32[4,6,1,128]{3,2,1,0:T(1,128)S(1)}, f32[4,6,1,128]{3,2,1,0:T(1,128)S(1)}, u32[]{:S(2)}, u32[]{:S(2)}) collective-permute-start(f32[4,6,1,128]{3,2,1,0:T(1,128)S(1)} %get-tuple-element.116), channel_id=1, source_target_pairs={{0,1},{1,2},{2,3},{4,5},{5,6},{6,7},{8,9},{9,10},{10,11},{12,13},{... | collective-permute-start | bytes 36872 | tf_op jit(solution)/shard_map/ppermute | solution.py:20
  129.3 5.9 collective-permute-start.16
  138.0 6.0 %collective-permute-start.18 = (f32[4,6,1,128]{3,2,1,0:T(1,128)S(1)}, f32[4,6,1,128]{3,2,1,0:T(1,128)S(1)}, u32[]{:S(2)}, u32[]{:S(2)}) collective-permute-start(f32[4,6,1,128]{3,2,1,0:T(1,128)S(1)} %get-tuple-element.114), channel_id=1, source_target_pairs={{0,1},{1,2},{2,3},{4,5},{5,6},{6,7},{8,9},{9,10},{10,11},{12,13},{... | collective-permute-start | bytes 36872 | tf_op jit(solution)/shard_map/ppermute | solution.py:20
  153.2 5.8 collective-permute-start.20
  162.4 6.0 %collective-permute-start.22 = (f32[4,6,1,128]{3,2,1,0:T(1,128)}, f32[4,6,1,128]{3,2,1,0:T(1,128)}, u32[]{:S(2)}, u32[]{:S(2)}) collective-permute-start(f32[4,6,1,128]{3,2,1,0:T(1,128)} %get-tuple-element.112), channel_id=1, source_target_pairs={{0,1},{1,2},{2,3},{4,5},{5,6},{6,7},{8,9},{9,10},{10,11},{12,13},{... | collective-permute-start | bytes 36872 | tf_op jit(solution)/shard_map/ppermute | solution.py:20
  179.5 6.0 %collective-permute-start.26 = (f32[4,6,1,128]{3,2,1,0:T(1,128)S(1)}, f32[4,6,1,128]{3,2,1,0:T(1,128)S(1)}, u32[]{:S(2)}, u32[]{:S(2)}) collective-permute-start(f32[4,6,1,128]{3,2,1,0:T(1,128)S(1)} %get-tuple-element.110), channel_id=1, source_target_pairs={{0,1},{1,2},{2,3},{4,5},{5,6},{6,7},{8,9},{9,10},{10,11},{12,13},{... | collective-permute-start | bytes 36872 | tf_op jit(solution)/shard_map/ppermute | solution.py:20
  196.6 6.0 %collective-permute-start.30 = (f32[4,6,1,128]{3,2,1,0:T(1,128)S(1)}, f32[4,6,1,128]{3,2,1,0:T(1,128)S(1)}, u32[]{:S(2)}, u32[]{:S(2)}) collective-permute-start(f32[4,6,1,128]{3,2,1,0:T(1,128)S(1)} %get-tuple-element.108), channel_id=1, source_target_pairs={{0,1},{1,2},{2,3},{4,5},{5,6},{6,7},{8,9},{9,10},{10,11},{12,13},{... | collective-permute-start | bytes 36872 | tf_op jit(solution)/shard_map/ppermute | solution.py:20
  204.6 6.0 %collective-permute-start.34 = (f32[4,6,1,128]{3,2,1,0:T(1,128)S(1)}, f32[4,6,1,128]{3,2,1,0:T(1,128)S(1)}, u32[]{:S(2)}, u32[]{:S(2)}) collective-permute-start(f32[4,6,1,128]{3,2,1,0:T(1,128)S(1)} %get-tuple-element.106), channel_id=1, source_target_pairs={{0,1},{1,2},{2,3},{4,5},{5,6},{6,7},{8,9},{9,10},{10,11},{12,13},{... | collective-permute-start | bytes 36872 | tf_op jit(solution)/shard_map/ppermute | solution.py:20
  212.4 144.6 %psum.14 = f32[4,128]{1,0:T(4,128)S(1)} all-reduce(f32[4,128]{1,0:T(4,128)S(1)} %fusion.300), channel_id=1, replica_groups=mesh['src'=8,'gx'=16,'gy'=4] {'gx','gy'}, use_global_device_ids=true, to_apply=%region_0.1 | all-reduce | flops 512 | bytes 4096 | tf_op jit(solution)/shard_map/psum | solution.py:140
  382.5 6.0 %collective-permute-start.42 = (f32[4,6,1,128]{3,2,1,0:T(1,128)S(1)}, f32[4,6,1,128]{3,2,1,0:T(1,128)S(1)}, u32[]{:S(2)}, u32[]{:S(2)}) collective-permute-start(f32[4,6,1,128]{3,2,1,0:T(1,128)S(1)} %get-tuple-element.102), channel_id=1, source_target_pairs={{0,1},{1,2},{2,3},{4,5},{5,6},{6,7},{8,9},{9,10},{10,11},{12,13},{... | collective-permute-start | bytes 36872 | tf_op jit(solution)/shard_map/ppermute | solution.py:20
  398.5 6.2 %collective-permute-start.46 = (f32[4,6,1,128]{3,2,1,0:T(1,128)S(1)}, f32[4,6,1,128]{3,2,1,0:T(1,128)S(1)}, u32[]{:S(2)}, u32[]{:S(2)}) collective-permute-start(f32[4,6,1,128]{3,2,1,0:T(1,128)S(1)} %get-tuple-element.100), channel_id=1, source_target_pairs={{0,1},{1,2},{2,3},{4,5},{5,6},{6,7},{8,9},{9,10},{10,11},{12,13},{... | collective-permute-start | bytes 36872 | tf_op jit(solution)/shard_map/ppermute | solution.py:20
  407.5 5.9 collective-permute-start.48
  416.3 6.0 %collective-permute-start.50 = (f32[4,6,1,128]{3,2,1,0:T(1,128)S(1)}, f32[4,6,1,128]{3,2,1,0:T(1,128)S(1)}, u32[]{:S(2)}, u32[]{:S(2)}) collective-permute-start(f32[4,6,1,128]{3,2,1,0:T(1,128)S(1)} %get-tuple-element.98), channel_id=1, source_target_pairs={{0,1},{1,2},{2,3},{4,5},{5,6},{6,7},{8,9},{9,10},{10,11},{12,13},{... | collective-permute-start | bytes 36872 | tf_op jit(solution)/shard_map/ppermute | solution.py:20
  425.3 5.6 collective-permute-start.52
  433.7 6.0 %collective-permute-start.54 = (f32[4,6,1,128]{3,2,1,0:T(1,128)S(1)}, f32[4,6,1,128]{3,2,1,0:T(1,128)S(1)}, u32[]{:S(2)}, u32[]{:S(2)}) collective-permute-start(f32[4,6,1,128]{3,2,1,0:T(1,128)S(1)} %get-tuple-element.96), channel_id=1, source_target_pairs={{0,1},{1,2},{2,3},{4,5},{5,6},{6,7},{8,9},{9,10},{10,11},{12,13},{... | collective-permute-start | bytes 36872 | tf_op jit(solution)/shard_map/ppermute | solution.py:20
  451.2 6.0 %collective-permute-start.58 = (f32[4,6,1,128]{3,2,1,0:T(1,128)S(1)}, f32[4,6,1,128]{3,2,1,0:T(1,128)S(1)}, u32[]{:S(2)}, u32[]{:S(2)}) collective-permute-start(f32[4,6,1,128]{3,2,1,0:T(1,128)S(1)} %get-tuple-element.94), channel_id=1, source_target_pairs={{0,1},{1,2},{2,3},{4,5},{5,6},{6,7},{8,9},{9,10},{10,11},{12,13},{... | collective-permute-start | bytes 36872 | tf_op jit(solution)/shard_map/ppermute | solution.py:20
  460.4 5.7 collective-permute-start.60
  469.2 6.0 %collective-permute-start.62 = (f32[8,6,1,128]{3,2,1,0:T(1,128)S(1)}, f32[8,6,1,128]{3,2,1,0:T(1,128)S(1)}, u32[]{:S(2)}, u32[]{:S(2)}) collective-permute-start(f32[8,6,1,128]{3,2,1,0:T(1,128)S(1)} %get-tuple-element.82), channel_id=1, source_target_pairs={{0,1},{1,2},{2,3},{4,5},{5,6},{6,7},{8,9},{9,10},{10,11},{12,13},{... | collective-permute-start | bytes 73736 | tf_op jit(solution)/shard_map/ppermute | solution.py:20
  477.8 106.1 %all-reduce.21.cloned.1.call-done = f32[4,32,128]{2,1,0:T(8,128)} async-done(((f32[4,32,128]{2,1,0:T(8,128)}), f32[4,32,128]{2,1,0:T(8,128)}) %all-reduce.21.cloned.1.call-update) | async-done | bytes 65552 | tf_op jit(solution)/shard_map/psum | solution.py:99
  (243 shorter events, 157.2 us)
Async XLA Ops:
  6.5 577.4 %all-reduce.21.cloned.1.call-start = ((), (), s32[]{:S(2)}) async-start(), calls=%async_computation | async-start | bytes 131072 | tf_op jit(solution)/shard_map/psum | solution.py:99
  36.5 13.1 %collective-permute-start.1 = (f32[1,1,32,128]{2,1,3,0:T(1,128)S(1)}, f32[1,1,32,128]{2,1,3,0:T(1,128)S(1)}, u32[]{:S(2)}, u32[]{:S(2)}) collective-permute-start(f32[1,1,32,128]{2,1,3,0:T(1,128)S(1)} %get-tuple-element.153), channel_id=1, source_target_pairs={{4,0},{8,4},{12,8},{16,12},{20,16},{24,20},{28,24},{32,28},{36,32}... | collective-permute-start | bytes 49160 | tf_op jit(solution)/shard_map/ppermute | solution.py:23
  37.8 11.8 %collective-permute-start = (f32[1,1,32,128]{2,1,3,0:T(1,128)S(1)}, f32[1,1,32,128]{2,1,3,0:T(1,128)S(1)}, u32[]{:S(2)}, u32[]{:S(2)}) collective-permute-start(f32[1,1,32,128]{2,1,3,0:T(1,128)S(1)} %get-tuple-element.152), channel_id=1, source_target_pairs={{0,4},{4,8},{8,12},{12,16},{16,20},{20,24},{24,28},{28,32},{32,36}... | collective-permute-start | bytes 49160 | tf_op jit(solution)/shard_map/ppermute | solution.py:20
  40.9 41.4 %collective-permute-start.4 = (f32[4,1,32,128]{3,2,1,0:T(8,128)S(1)}, f32[4,1,32,128]{3,2,1,0:T(8,128)S(1)}, u32[]{:S(2)}, u32[]{:S(2)}) collective-permute-start(f32[4,1,32,128]{3,2,1,0:T(8,128)S(1)} %get-tuple-element.151), channel_id=1, source_target_pairs={{0,4},{4,8},{8,12},{12,16},{16,20},{20,24},{24,28},{28,32},{32,36}... | collective-permute-start | bytes 196616 | tf_op jit(solution)/shard_map/ppermute | solution.py:20
  44.8 37.5 %collective-permute-start.5 = (f32[4,1,32,128]{3,2,1,0:T(8,128)S(1)}, f32[4,1,32,128]{3,2,1,0:T(8,128)S(1)}, u32[]{:S(2)}, u32[]{:S(2)}) collective-permute-start(f32[4,1,32,128]{3,2,1,0:T(8,128)S(1)} %get-tuple-element.150), channel_id=1, source_target_pairs={{4,0},{8,4},{12,8},{16,12},{20,16},{24,20},{28,24},{32,28},{36,32}... | collective-permute-start | bytes 196616 | tf_op jit(solution)/shard_map/ppermute | solution.py:23
  50.0 29.9 %collective-permute-start.3 = (f32[1,6,1,128]{2,1,3,0:T(8,128)S(1)}, f32[1,6,1,128]{2,1,3,0:T(8,128)S(1)}, u32[]{:S(2)}, u32[]{:S(2)}) collective-permute-start(f32[1,6,1,128]{2,1,3,0:T(8,128)S(1)} %get-tuple-element.93), channel_id=1, source_target_pairs={{1,0},{2,1},{3,2},{5,4},{6,5},{7,6},{9,8},{10,9},{11,10},{13,12},{... | collective-permute-start | bytes 9224 | tf_op jit(solution)/shard_map/ppermute | solution.py:23
  55.4 24.5 %collective-permute-start.2 = (f32[1,6,1,128]{2,1,3,0:T(8,128)S(1)}, f32[1,6,1,128]{2,1,3,0:T(8,128)S(1)}, u32[]{:S(2)}, u32[]{:S(2)}) collective-permute-start(f32[1,6,1,128]{2,1,3,0:T(8,128)S(1)} %get-tuple-element.92), channel_id=1, source_target_pairs={{0,1},{1,2},{2,3},{4,5},{5,6},{6,7},{8,9},{9,10},{10,11},{12,13},{... | collective-permute-start | bytes 9224 | tf_op jit(solution)/shard_map/ppermute | solution.py:20
  82.3 11.8 %collective-permute-start.7 = (f32[4,6,1,128]{3,2,1,0:T(1,128)S(1)}, f32[4,6,1,128]{3,2,1,0:T(1,128)S(1)}, u32[]{:S(2)}, u32[]{:S(2)}) collective-permute-start(f32[4,6,1,128]{3,2,1,0:T(1,128)S(1)} %get-tuple-element.121), channel_id=1, source_target_pairs={{1,0},{2,1},{3,2},{5,4},{6,5},{7,6},{9,8},{10,9},{11,10},{13,12},{... | collective-permute-start | bytes 36872 | tf_op jit(solution)/shard_map/ppermute | solution.py:23
  84.7 9.4 %collective-permute-start.6 = (f32[4,6,1,128]{3,2,1,0:T(1,128)S(1)}, f32[4,6,1,128]{3,2,1,0:T(1,128)S(1)}, u32[]{:S(2)}, u32[]{:S(2)}) collective-permute-start(f32[4,6,1,128]{3,2,1,0:T(1,128)S(1)} %get-tuple-element.120), channel_id=1, source_target_pairs={{0,1},{1,2},{2,3},{4,5},{5,6},{6,7},{8,9},{9,10},{10,11},{12,13},{... | collective-permute-start | bytes 36872 | tf_op jit(solution)/shard_map/ppermute | solution.py:20
  100.5 8.0 %collective-permute-start.11 = (f32[4,6,1,128]{3,2,1,0:T(1,128)S(1)}, f32[4,6,1,128]{3,2,1,0:T(1,128)S(1)}, u32[]{:S(2)}, u32[]{:S(2)}) collective-permute-start(f32[4,6,1,128]{3,2,1,0:T(1,128)S(1)} %get-tuple-element.119), channel_id=1, source_target_pairs={{1,0},{2,1},{3,2},{5,4},{6,5},{7,6},{9,8},{10,9},{11,10},{13,12},{... | collective-permute-start | bytes 36872 | tf_op jit(solution)/shard_map/ppermute | solution.py:23
  118.2 8.0 %collective-permute-start.15 = (f32[4,6,1,128]{3,2,1,0:T(1,128)S(1)}, f32[4,6,1,128]{3,2,1,0:T(1,128)S(1)}, u32[]{:S(2)}, u32[]{:S(2)}) collective-permute-start(f32[4,6,1,128]{3,2,1,0:T(1,128)S(1)} %get-tuple-element.117), channel_id=1, source_target_pairs={{1,0},{2,1},{3,2},{5,4},{6,5},{7,6},{9,8},{10,9},{11,10},{13,12},{... | collective-permute-start | bytes 36872 | tf_op jit(solution)/shard_map/ppermute | solution.py:23
  136.1 15.5 %collective-permute-start.19 = (f32[4,6,1,128]{3,2,1,0:T(1,128)S(1)}, f32[4,6,1,128]{3,2,1,0:T(1,128)S(1)}, u32[]{:S(2)}, u32[]{:S(2)}) collective-permute-start(f32[4,6,1,128]{3,2,1,0:T(1,128)S(1)} %get-tuple-element.115), channel_id=1, source_target_pairs={{1,0},{2,1},{3,2},{5,4},{6,5},{7,6},{9,8},{10,9},{11,10},{13,12},{... | collective-permute-start | bytes 36872 | tf_op jit(solution)/shard_map/ppermute | solution.py:23
  138.0 13.6 %collective-permute-start.18 = (f32[4,6,1,128]{3,2,1,0:T(1,128)S(1)}, f32[4,6,1,128]{3,2,1,0:T(1,128)S(1)}, u32[]{:S(2)}, u32[]{:S(2)}) collective-permute-start(f32[4,6,1,128]{3,2,1,0:T(1,128)S(1)} %get-tuple-element.114), channel_id=1, source_target_pairs={{0,1},{1,2},{2,3},{4,5},{5,6},{6,7},{8,9},{9,10},{10,11},{12,13},{... | collective-permute-start | bytes 36872 | tf_op jit(solution)/shard_map/ppermute | solution.py:20
  144.7 32.0 %collective-permute-start.32 = (f32[4,1,32,128]{3,2,1,0:T(8,128)}, f32[4,1,32,128]{3,2,1,0:T(8,128)S(1)}, u32[]{:S(2)}, u32[]{:S(2)}) collective-permute-start(f32[4,1,32,128]{3,2,1,0:T(8,128)} %get-tuple-element.137), channel_id=1, source_target_pairs={{0,4},{4,8},{8,12},{12,16},{16,20},{20,24},{24,28},{28,32},{32,36}... | collective-permute-start | bytes 196616 | tf_op jit(solution)/shard_map/ppermute | solution.py:20
  150.2 43.6 %collective-permute-start.33 = (f32[4,1,32,128]{3,2,1,0:T(8,128)}, f32[4,1,32,128]{3,2,1,0:T(8,128)}, u32[]{:S(2)}, u32[]{:S(2)}) collective-permute-start(f32[4,1,32,128]{3,2,1,0:T(8,128)} %get-tuple-element.136), channel_id=1, source_target_pairs={{4,0},{8,4},{12,8},{16,12},{20,16},{24,20},{28,24},{32,28},{36,32}... | collective-permute-start | bytes 196616 | tf_op jit(solution)/shard_map/ppermute | solution.py:23
  160.5 9.8 %collective-permute-start.23 = (f32[4,6,1,128]{3,2,1,0:T(1,128)}, f32[4,6,1,128]{3,2,1,0:T(1,128)}, u32[]{:S(2)}, u32[]{:S(2)}) collective-permute-start(f32[4,6,1,128]{3,2,1,0:T(1,128)} %get-tuple-element.113), channel_id=1, source_target_pairs={{1,0},{2,1},{3,2},{5,4},{6,5},{7,6},{9,8},{10,9},{11,10},{13,12},{... | collective-permute-start | bytes 36872 | tf_op jit(solution)/shard_map/ppermute | solution.py:23
  177.6 8.0 %collective-permute-start.27 = (f32[4,6,1,128]{3,2,1,0:T(1,128)S(1)}, f32[4,6,1,128]{3,2,1,0:T(1,128)S(1)}, u32[]{:S(2)}, u32[]{:S(2)}) collective-permute-start(f32[4,6,1,128]{3,2,1,0:T(1,128)S(1)} %get-tuple-element.111), channel_id=1, source_target_pairs={{1,0},{2,1},{3,2},{5,4},{6,5},{7,6},{9,8},{10,9},{11,10},{13,12},{... | collective-permute-start | bytes 36872 | tf_op jit(solution)/shard_map/ppermute | solution.py:23
  194.7 16.0 %collective-permute-start.31 = (f32[4,6,1,128]{3,2,1,0:T(1,128)S(1)}, f32[4,6,1,128]{3,2,1,0:T(1,128)S(1)}, u32[]{:S(2)}, u32[]{:S(2)}) collective-permute-start(f32[4,6,1,128]{3,2,1,0:T(1,128)S(1)} %get-tuple-element.109), channel_id=1, source_target_pairs={{1,0},{2,1},{3,2},{5,4},{6,5},{7,6},{9,8},{10,9},{11,10},{13,12},{... | collective-permute-start | bytes 36872 | tf_op jit(solution)/shard_map/ppermute | solution.py:23
  196.6 14.0 %collective-permute-start.30 = (f32[4,6,1,128]{3,2,1,0:T(1,128)S(1)}, f32[4,6,1,128]{3,2,1,0:T(1,128)S(1)}, u32[]{:S(2)}, u32[]{:S(2)}) collective-permute-start(f32[4,6,1,128]{3,2,1,0:T(1,128)S(1)} %get-tuple-element.108), channel_id=1, source_target_pairs={{0,1},{1,2},{2,3},{4,5},{5,6},{6,7},{8,9},{9,10},{10,11},{12,13},{... | collective-permute-start | bytes 36872 | tf_op jit(solution)/shard_map/ppermute | solution.py:20
  202.7 154.8 %collective-permute-start.35 = (f32[4,6,1,128]{3,2,1,0:T(1,128)S(1)}, f32[4,6,1,128]{3,2,1,0:T(1,128)S(1)}, u32[]{:S(2)}, u32[]{:S(2)}) collective-permute-start(f32[4,6,1,128]{3,2,1,0:T(1,128)S(1)} %get-tuple-element.107), channel_id=1, source_target_pairs={{1,0},{2,1},{3,2},{5,4},{6,5},{7,6},{9,8},{10,9},{11,10},{13,12},{... | collective-permute-start | bytes 36872 | tf_op jit(solution)/shard_map/ppermute | solution.py:23
  204.6 152.9 %collective-permute-start.34 = (f32[4,6,1,128]{3,2,1,0:T(1,128)S(1)}, f32[4,6,1,128]{3,2,1,0:T(1,128)S(1)}, u32[]{:S(2)}, u32[]{:S(2)}) collective-permute-start(f32[4,6,1,128]{3,2,1,0:T(1,128)S(1)} %get-tuple-element.106), channel_id=1, source_target_pairs={{0,1},{1,2},{2,3},{4,5},{5,6},{6,7},{8,9},{9,10},{10,11},{12,13},{... | collective-permute-start | bytes 36872 | tf_op jit(solution)/shard_map/ppermute | solution.py:20
  396.6 8.2 %collective-permute-start.47 = (f32[4,6,1,128]{3,2,1,0:T(1,128)S(1)}, f32[4,6,1,128]{3,2,1,0:T(1,128)S(1)}, u32[]{:S(2)}, u32[]{:S(2)}) collective-permute-start(f32[4,6,1,128]{3,2,1,0:T(1,128)S(1)} %get-tuple-element.101), channel_id=1, source_target_pairs={{1,0},{2,1},{3,2},{5,4},{6,5},{7,6},{9,8},{10,9},{11,10},{13,12},{... | collective-permute-start | bytes 36872 | tf_op jit(solution)/shard_map/ppermute | solution.py:23
  414.3 8.0 %collective-permute-start.51 = (f32[4,6,1,128]{3,2,1,0:T(1,128)S(1)}, f32[4,6,1,128]{3,2,1,0:T(1,128)S(1)}, u32[]{:S(2)}, u32[]{:S(2)}) collective-permute-start(f32[4,6,1,128]{3,2,1,0:T(1,128)S(1)} %get-tuple-element.99), channel_id=1, source_target_pairs={{1,0},{2,1},{3,2},{5,4},{6,5},{7,6},{9,8},{10,9},{11,10},{13,12},{... | collective-permute-start | bytes 36872 | tf_op jit(solution)/shard_map/ppermute | solution.py:23
  467.2 8.8 %collective-permute-start.63 = (f32[8,6,1,128]{3,2,1,0:T(1,128)S(1)}, f32[8,6,1,128]{3,2,1,0:T(1,128)S(1)}, u32[]{:S(2)}, u32[]{:S(2)}) collective-permute-start(f32[8,6,1,128]{3,2,1,0:T(1,128)S(1)} %get-tuple-element.83), channel_id=1, source_target_pairs={{1,0},{2,1},{3,2},{5,4},{6,5},{7,6},{9,8},{10,9},{11,10},{13,12},{... | collective-permute-start | bytes 73736 | tf_op jit(solution)/shard_map/ppermute | solution.py:23
  (62 other events, 980.0 us)
Sparse Core Ops, SparseCore 0:
  477.9 105.9 all-reduce.20
where the time goes:
time: 595 us; the launch traced here: 592 us
  starting transfers between devices  224 us (38%)
  blocking collectives  174 us (29%)
  waiting for transfers between devices  153 us (26%)
  other arithmetic  15 us (3%)
  between operations  14.6 us (2%)
  local copies, waits for them, and re-layouts  12.1 us (2%)
    ppermute x32, starting transfers between devices, padded_2(): lax.ppermute(lax.slice_in_dim(block, block.shape[dim] - width, None, axis...  166 us
    psum x1, blocking collectives, body(): predicted = lax.psum(local_values, ('gx', 'gy'))  145 us
    psum x1, waiting for transfers between devices, reduce_groups(): summed = lax.psum(partial_value, 'src')  106 us
    ppermute x32, starting transfers between devices, padded_2(): lax.ppermute(lax.slice_in_dim(block, 0, width, axis=dim), axis, backward)  58.2 us
    all_gather x1, blocking collectives, body(): panel = lax.all_gather(conductivity, 'src', axis=2, tiled=True)  29 us
    ppermute x32, waiting for transfers between devices, padded_2(): lax.ppermute(lax.slice_in_dim(block, block.shape[dim] - width, None, axis...  24.7 us
    ppermute x32, waiting for transfers between devices, padded_2(): lax.ppermute(lax.slice_in_dim(block, 0, width, axis=dim), axis, backward)  22 us
  transfers between devices with their start and end apart: 65, of which 24 were waited for; matrix products, arithmetic and copies ran while one was open for 3% of the time, Pallas kernels for 0%

commit v1 on v0

--- a/solution.py
+++ b/solution.py
@@ -137,7 +137,7 @@
     local_values = jnp.dot(
         top, pickup.T, precision=lax.Precision.HIGHEST, preferred_element_type=jnp.float32
     )
-    predicted = lax.psum(local_values, ("gx", "gy"))
+    predicted = jax.lax.psum(jax.lax.psum(local_values, "gy"), "gx")
     misfit = predicted - rows_observed
     back = jnp.dot(
         misfit, pickup, precision=lax.Precision.HIGHEST, preferred_element_type=jnp.float32

time: 595 us -> 488 us (0.82)
  blocking collectives: 174 us -> 72.3 us
  waiting for transfers between devices: 153 us -> 146 us
    psum x1 -> x2, blocking collectives: 145 us -> 43.3 us  [body(): predicted = jax.lax.psum(jax.lax.psum(local_values, 'gy'), 'gx')]
    psum x1, waiting for transfers between devices: 106 us -> 99.9 us  [reduce_groups(): summed = lax.psum(partial_value, 'src')]
where the time goes in v1:
time: 488 us; the launch traced here: 486 us
  starting transfers between devices  225 us (46%)
  waiting for transfers between devices  146 us (30%)
  blocking collectives  72.3 us (15%)
  other arithmetic  15 us (3%)
  between operations  14.6 us (3%)
  local copies, waits for them, and re-layouts  12.1 us (2%)
    ppermute x32, starting transfers between devices, padded_2(): lax.ppermute(lax.slice_in_dim(block, block.shape[dim] - width, None, axis...  167 us
    psum x1, waiting for transfers between devices, reduce_groups(): summed = lax.psum(partial_value, 'src')  99.9 us
    ppermute x32, starting transfers between devices, padded_2(): lax.ppermute(lax.slice_in_dim(block, 0, width, axis=dim), axis, backward)  58 us
    psum x2, blocking collectives, body(): predicted = jax.lax.psum(jax.lax.psum(local_values, 'gy'), 'gx')  43.3 us
    all_gather x1, blocking collectives, body(): panel = lax.all_gather(conductivity, 'src', axis=2, tiled=True)  29 us
    ppermute x32, waiting for transfers between devices, padded_2(): lax.ppermute(lax.slice_in_dim(block, block.shape[dim] - width, None, axis...  24.5 us
    ppermute x32, waiting for transfers between devices, padded_2(): lax.ppermute(lax.slice_in_dim(block, 0, width, axis=dim), axis, backward)  22 us
  transfers between devices with their start and end apart: 65, of which 24 were waited for; matrix products, arithmetic and copies ran while one was open for 3% of the time, Pallas kernels for 0%

profile of v1, /device:TPU:16, one launch (start us, length us, event | category | flops | bytes accessed | tf_op | source)
XLA Modules:
  0.0 486.2 jit_solution(8355135717633112644)
XLA Ops:
  7.3 29.0 %all_gather.3 = f32[4,32,128]{1,0,2:T(4,128)S(1)} all-gather(f32[4,32,16]{1,0,2:T(4,128)S(1)} %copy.69), channel_id=1, replica_groups=mesh['src'=8,'gx'=16,'gy'=4] {'src'}, dimensions={2}, use_global_device_ids=true | all-gather | bytes 73728 | tf_op jit(solution)/shard_map/all_gather | solution.py:104
  58.0 21.9 %collective-permute-done.3 = f32[1,6,1,128]{2,1,3,0:T(8,128)S(1)} collective-permute-done((f32[1,6,1,128]{2,1,3,0:T(8,128)S(1)}, f32[1,6,1,128]{2,1,3,0:T(8,128)S(1)}, u32[]{:S(2)}, u32[]{:S(2)}) %collective-permute-start.3) | collective-permute-done | bytes 3104 | tf_op jit(solution)/shard_map/ppermute | solution.py:23
  102.4 6.0 %collective-permute-start.10 = (f32[4,6,1,128]{3,2,1,0:T(1,128)S(1)}, f32[4,6,1,128]{3,2,1,0:T(1,128)S(1)}, u32[]{:S(2)}, u32[]{:S(2)}) collective-permute-start(f32[4,6,1,128]{3,2,1,0:T(1,128)S(1)} %get-tuple-element.118), channel_id=1, source_target_pairs={{0,1},{1,2},{2,3},{4,5},{5,6},{6,7},{8,9},{9,10},{10,11},{12,13},{... | collective-permute-start | bytes 36872 | tf_op jit(solution)/shard_map/ppermute | solution.py:20
  111.4 5.8 %collective-permute-start.12 = (f32[4,1,32,128]{3,2,1,0:T(8,128)S(1)}, f32[4,1,32,128]{3,2,1,0:T(8,128)S(1)}, u32[]{:S(2)}, u32[]{:S(2)}) collective-permute-start(f32[4,1,32,128]{3,2,1,0:T(8,128)S(1)} %get-tuple-element.146), channel_id=1, source_target_pairs={{0,4},{4,8},{8,12},{12,16},{16,20},{20,24},{24,28},{28,32},{32,36}... | collective-permute-start | bytes 196616 | tf_op jit(solution)/shard_map/ppermute | solution.py:20
  120.1 6.0 %collective-permute-start.14 = (f32[4,6,1,128]{3,2,1,0:T(1,128)S(1)}, f32[4,6,1,128]{3,2,1,0:T(1,128)S(1)}, u32[]{:S(2)}, u32[]{:S(2)}) collective-permute-start(f32[4,6,1,128]{3,2,1,0:T(1,128)S(1)} %get-tuple-element.116), channel_id=1, source_target_pairs={{0,1},{1,2},{2,3},{4,5},{5,6},{6,7},{8,9},{9,10},{10,11},{12,13},{... | collective-permute-start | bytes 36872 | tf_op jit(solution)/shard_map/ppermute | solution.py:20
  129.3 5.9 %collective-permute-start.16 = (f32[4,1,32,128]{3,2,1,0:T(8,128)S(1)}, f32[4,1,32,128]{3,2,1,0:T(8,128)S(1)}, u32[]{:S(2)}, u32[]{:S(2)}) collective-permute-start(f32[4,1,32,128]{3,2,1,0:T(8,128)S(1)} %get-tuple-element.144), channel_id=1, source_target_pairs={{0,4},{4,8},{8,12},{12,16},{16,20},{20,24},{24,28},{28,32},{32,36}... | collective-permute-start | bytes 196616 | tf_op jit(solution)/shard_map/ppermute | solution.py:20
  138.0 6.0 %collective-permute-start.18 = (f32[4,6,1,128]{3,2,1,0:T(1,128)S(1)}, f32[4,6,1,128]{3,2,1,0:T(1,128)S(1)}, u32[]{:S(2)}, u32[]{:S(2)}) collective-permute-start(f32[4,6,1,128]{3,2,1,0:T(1,128)S(1)} %get-tuple-element.114), channel_id=1, source_target_pairs={{0,1},{1,2},{2,3},{4,5},{5,6},{6,7},{8,9},{9,10},{10,11},{12,13},{... | collective-permute-start | bytes 36872 | tf_op jit(solution)/shard_map/ppermute | solution.py:20
  153.2 5.8 %collective-permute-start.20 = (f32[4,1,32,128]{3,2,1,0:T(8,128)S(1)}, f32[4,1,32,128]{3,2,1,0:T(8,128)S(1)}, u32[]{:S(2)}, u32[]{:S(2)}) collective-permute-start(f32[4,1,32,128]{3,2,1,0:T(8,128)S(1)} %get-tuple-element.142), channel_id=1, source_target_pairs={{0,4},{4,8},{8,12},{12,16},{16,20},{20,24},{24,28},{28,32},{32,36}... | collective-permute-start | bytes 196616 | tf_op jit(solution)/shard_map/ppermute | solution.py:20
  162.4 6.0 %collective-permute-start.22 = (f32[4,6,1,128]{3,2,1,0:T(1,128)}, f32[4,6,1,128]{3,2,1,0:T(1,128)}, u32[]{:S(2)}, u32[]{:S(2)}) collective-permute-start(f32[4,6,1,128]{3,2,1,0:T(1,128)} %get-tuple-element.112), channel_id=1, source_target_pairs={{0,1},{1,2},{2,3},{4,5},{5,6},{6,7},{8,9},{9,10},{10,11},{12,13},{... | collective-permute-start | bytes 36872 | tf_op jit(solution)/shard_map/ppermute | solution.py:20
  179.6 6.0 %collective-permute-start.26 = (f32[4,6,1,128]{3,2,1,0:T(1,128)S(1)}, f32[4,6,1,128]{3,2,1,0:T(1,128)S(1)}, u32[]{:S(2)}, u32[]{:S(2)}) collective-permute-start(f32[4,6,1,128]{3,2,1,0:T(1,128)S(1)} %get-tuple-element.110), channel_id=1, source_target_pairs={{0,1},{1,2},{2,3},{4,5},{5,6},{6,7},{8,9},{9,10},{10,11},{12,13},{... | collective-permute-start | bytes 36872 | tf_op jit(solution)/shard_map/ppermute | solution.py:20
  196.6 6.0 %collective-permute-start.30 = (f32[4,6,1,128]{3,2,1,0:T(1,128)S(1)}, f32[4,6,1,128]{3,2,1,0:T(1,128)S(1)}, u32[]{:S(2)}, u32[]{:S(2)}) collective-permute-start(f32[4,6,1,128]{3,2,1,0:T(1,128)S(1)} %get-tuple-element.108), channel_id=1, source_target_pairs={{0,1},{1,2},{2,3},{4,5},{5,6},{6,7},{8,9},{9,10},{10,11},{12,13},{... | collective-permute-start | bytes 36872 | tf_op jit(solution)/shard_map/ppermute | solution.py:20
  204.6 6.0 %collective-permute-start.34 = (f32[4,6,1,128]{3,2,1,0:T(1,128)S(1)}, f32[4,6,1,128]{3,2,1,0:T(1,128)S(1)}, u32[]{:S(2)}, u32[]{:S(2)}) collective-permute-start(f32[4,6,1,128]{3,2,1,0:T(1,128)S(1)} %get-tuple-element.106), channel_id=1, source_target_pairs={{0,1},{1,2},{2,3},{4,5},{5,6},{6,7},{8,9},{9,10},{10,11},{12,13},{... | collective-permute-start | bytes 36872 | tf_op jit(solution)/shard_map/ppermute | solution.py:20
  212.4 9.1 %psum.21 = f32[4,128]{1,0:T(4,128)S(1)} all-reduce(f32[4,128]{1,0:T(4,128)S(1)} %fusion.300), channel_id=1, replica_groups=mesh['src'=8,'gx'=16,'gy'=4] {'gy'}, use_global_device_ids=true, to_apply=%region_0.1 | all-reduce | flops 512 | bytes 4096 | tf_op jit(solution)/shard_map/psum | solution.py:140
  221.5 34.1 %psum.22 = f32[4,128]{1,0:T(4,128)S(1)} all-reduce(f32[4,128]{1,0:T(4,128)S(1)} %psum.21), channel_id=1, replica_groups=mesh['src'=8,'gx'=16,'gy'=4] {'gx'}, use_global_device_ids=true, to_apply=%region_1.2 | all-reduce | flops 512 | bytes 4096 | tf_op jit(solution)/shard_map/psum | solution.py:140
  281.0 6.0 %collective-permute-start.42 = (f32[4,6,1,128]{3,2,1,0:T(1,128)S(1)}, f32[4,6,1,128]{3,2,1,0:T(1,128)S(1)}, u32[]{:S(2)}, u32[]{:S(2)}) collective-permute-start(f32[4,6,1,128]{3,2,1,0:T(1,128)S(1)} %get-tuple-element.102), channel_id=1, source_target_pairs={{0,1},{1,2},{2,3},{4,5},{5,6},{6,7},{8,9},{9,10},{10,11},{12,13},{... | collective-permute-start | bytes 36872 | tf_op jit(solution)/shard_map/ppermute | solution.py:20
  290.0 5.8 %collective-permute-start.44 = (f32[4,1,32,128]{3,2,1,0:T(8,128)S(1)}, f32[4,1,32,128]{3,2,1,0:T(8,128)S(1)}, u32[]{:S(2)}, u32[]{:S(2)}) collective-permute-start(f32[4,1,32,128]{3,2,1,0:T(8,128)S(1)} %get-tuple-element.130), channel_id=1, source_target_pairs={{0,4},{4,8},{8,12},{12,16},{16,20},{20,24},{24,28},{28,32},{32,36}... | collective-permute-start | bytes 196616 | tf_op jit(solution)/shard_map/ppermute | solution.py:20
  298.5 6.0 %collective-permute-start.46 = (f32[4,6,1,128]{3,2,1,0:T(1,128)S(1)}, f32[4,6,1,128]{3,2,1,0:T(1,128)S(1)}, u32[]{:S(2)}, u32[]{:S(2)}) collective-permute-start(f32[4,6,1,128]{3,2,1,0:T(1,128)S(1)} %get-tuple-element.100), channel_id=1, source_target_pairs={{0,1},{1,2},{2,3},{4,5},{5,6},{6,7},{8,9},{9,10},{10,11},{12,13},{... | collective-permute-start | bytes 36872 | tf_op jit(solution)/shard_map/ppermute | solution.py:20
  307.5 5.9 %collective-permute-start.48 = (f32[4,1,32,128]{3,2,1,0:T(8,128)S(1)}, f32[4,1,32,128]{3,2,1,0:T(8,128)S(1)}, u32[]{:S(2)}, u32[]{:S(2)}) collective-permute-start(f32[4,1,32,128]{3,2,1,0:T(8,128)S(1)} %get-tuple-element.128), channel_id=1, source_target_pairs={{0,4},{4,8},{8,12},{12,16},{16,20},{20,24},{24,28},{28,32},{32,36}... | collective-permute-start | bytes 196616 | tf_op jit(solution)/shard_map/ppermute | solution.py:20
  316.2 6.0 %collective-permute-start.50 = (f32[4,6,1,128]{3,2,1,0:T(1,128)S(1)}, f32[4,6,1,128]{3,2,1,0:T(1,128)S(1)}, u32[]{:S(2)}, u32[]{:S(2)}) collective-permute-start(f32[4,6,1,128]{3,2,1,0:T(1,128)S(1)} %get-tuple-element.98), channel_id=1, source_target_pairs={{0,1},{1,2},{2,3},{4,5},{5,6},{6,7},{8,9},{9,10},{10,11},{12,13},{... | collective-permute-start | bytes 36872 | tf_op jit(solution)/shard_map/ppermute | solution.py:20
  333.7 6.0 %collective-permute-start.54 = (f32[4,6,1,128]{3,2,1,0:T(1,128)S(1)}, f32[4,6,1,128]{3,2,1,0:T(1,128)S(1)}, u32[]{:S(2)}, u32[]{:S(2)}) collective-permute-start(f32[4,6,1,128]{3,2,1,0:T(1,128)S(1)} %get-tuple-element.96), channel_id=1, source_target_pairs={{0,1},{1,2},{2,3},{4,5},{5,6},{6,7},{8,9},{9,10},{10,11},{12,13},{... | collective-permute-start | bytes 36872 | tf_op jit(solution)/shard_map/ppermute | solution.py:20
  351.2 6.0 %collective-permute-start.58 = (f32[4,6,1,128]{3,2,1,0:T(1,128)S(1)}, f32[4,6,1,128]{3,2,1,0:T(1,128)S(1)}, u32[]{:S(2)}, u32[]{:S(2)}) collective-permute-start(f32[4,6,1,128]{3,2,1,0:T(1,128)S(1)} %get-tuple-element.94), channel_id=1, source_target_pairs={{0,1},{1,2},{2,3},{4,5},{5,6},{6,7},{8,9},{9,10},{10,11},{12,13},{... | collective-permute-start | bytes 36872 | tf_op jit(solution)/shard_map/ppermute | solution.py:20
  360.4 5.7 %collective-permute-start.60 = (f32[8,1,32,128]{3,2,1,0:T(8,128)S(1)}, f32[8,1,32,128]{3,2,1,0:T(8,128)S(1)}, u32[]{:S(2)}, u32[]{:S(2)}) collective-permute-start(f32[8,1,32,128]{3,2,1,0:T(8,128)S(1)} %get-tuple-element.90), channel_id=1, source_target_pairs={{0,4},{4,8},{8,12},{12,16},{16,20},{20,24},{24,28},{28,32},{32,36}... | collective-permute-start | bytes 393224 | tf_op jit(solution)/shard_map/ppermute | solution.py:20
  369.2 6.0 %collective-permute-start.62 = (f32[8,6,1,128]{3,2,1,0:T(1,128)S(1)}, f32[8,6,1,128]{3,2,1,0:T(1,128)S(1)}, u32[]{:S(2)}, u32[]{:S(2)}) collective-permute-start(f32[8,6,1,128]{3,2,1,0:T(1,128)S(1)} %get-tuple-element.82), channel_id=1, source_target_pairs={{0,1},{1,2},{2,3},{4,5},{5,6},{6,7},{8,9},{9,10},{10,11},{12,13},{... | collective-permute-start | bytes 73736 | tf_op jit(solution)/shard_map/ppermute | solution.py:20
  377.8 99.9 %all-reduce.21.cloned.1.call-done = f32[4,32,128]{2,1,0:T(8,128)} async-done(((f32[4,32,128]{2,1,0:T(8,128)}), f32[4,32,128]{2,1,0:T(8,128)}) %all-reduce.21.cloned.1.call-update) | async-done | bytes 65552 | tf_op jit(solution)/shard_map/psum | solution.py:99
  (244 shorter events, 164.1 us)
Async XLA Ops:
  6.5 471.2 %all-reduce.21.cloned.1.call-start = ((), (), s32[]{:S(2)}) async-start(), calls=%async_computation | async-start | bytes 131072 | tf_op jit(solution)/shard_map/psum | solution.py:99
  36.5 13.1 %collective-permute-start.1 = (f32[1,1,32,128]{2,1,3,0:T(1,128)S(1)}, f32[1,1,32,128]{2,1,3,0:T(1,128)S(1)}, u32[]{:S(2)}, u32[]{:S(2)}) collective-permute-start(f32[1,1,32,128]{2,1,3,0:T(1,128)S(1)} %get-tuple-element.153), channel_id=1, source_target_pairs={{4,0},{8,4},{12,8},{16,12},{20,16},{24,20},{28,24},{32,28},{36,32}... | collective-permute-start | bytes 49160 | tf_op jit(solution)/shard_map/ppermute | solution.py:23
  37.8 11.8 %collective-permute-start = (f32[1,1,32,128]{2,1,3,0:T(1,128)S(1)}, f32[1,1,32,128]{2,1,3,0:T(1,128)S(1)}, u32[]{:S(2)}, u32[]{:S(2)}) collective-permute-start(f32[1,1,32,128]{2,1,3,0:T(1,128)S(1)} %get-tuple-element.152), channel_id=1, source_target_pairs={{0,4},{4,8},{8,12},{12,16},{16,20},{20,24},{24,28},{28,32},{32,36}... | collective-permute-start | bytes 49160 | tf_op jit(solution)/shard_map/ppermute | solution.py:20
  40.9 41.4 %collective-permute-start.4 = (f32[4,1,32,128]{3,2,1,0:T(8,128)S(1)}, f32[4,1,32,128]{3,2,1,0:T(8,128)S(1)}, u32[]{:S(2)}, u32[]{:S(2)}) collective-permute-start(f32[4,1,32,128]{3,2,1,0:T(8,128)S(1)} %get-tuple-element.151), channel_id=1, source_target_pairs={{0,4},{4,8},{8,12},{12,16},{16,20},{20,24},{24,28},{28,32},{32,36}... | collective-permute-start | bytes 196616 | tf_op jit(solution)/shard_map/ppermute | solution.py:20
  44.8 37.5 %collective-permute-start.5 = (f32[4,1,32,128]{3,2,1,0:T(8,128)S(1)}, f32[4,1,32,128]{3,2,1,0:T(8,128)S(1)}, u32[]{:S(2)}, u32[]{:S(2)}) collective-permute-start(f32[4,1,32,128]{3,2,1,0:T(8,128)S(1)} %get-tuple-element.150), channel_id=1, source_target_pairs={{4,0},{8,4},{12,8},{16,12},{20,16},{24,20},{28,24},{32,28},{36,32}... | collective-permute-start | bytes 196616 | tf_op jit(solution)/shard_map/ppermute | solution.py:23
  50.0 29.9 %collective-permute-start.3 = (f32[1,6,1,128]{2,1,3,0:T(8,128)S(1)}, f32[1,6,1,128]{2,1,3,0:T(8,128)S(1)}, u32[]{:S(2)}, u32[]{:S(2)}) collective-permute-start(f32[1,6,1,128]{2,1,3,0:T(8,128)S(1)} %get-tuple-element.93), channel_id=1, source_target_pairs={{1,0},{2,1},{3,2},{5,4},{6,5},{7,6},{9,8},{10,9},{11,10},{13,12},{... | collective-permute-start | bytes 9224 | tf_op jit(solution)/shard_map/ppermute | solution.py:23
  55.4 24.5 %collective-permute-start.2 = (f32[1,6,1,128]{2,1,3,0:T(8,128)S(1)}, f32[1,6,1,128]{2,1,3,0:T(8,128)S(1)}, u32[]{:S(2)}, u32[]{:S(2)}) collective-permute-start(f32[1,6,1,128]{2,1,3,0:T(8,128)S(1)} %get-tuple-element.92), channel_id=1, source_target_pairs={{0,1},{1,2},{2,3},{4,5},{5,6},{6,7},{8,9},{9,10},{10,11},{12,13},{... | collective-permute-start | bytes 9224 | tf_op jit(solution)/shard_map/ppermute | solution.py:20
  82.3 11.8 %collective-permute-start.7 = (f32[4,6,1,128]{3,2,1,0:T(1,128)S(1)}, f32[4,6,1,128]{3,2,1,0:T(1,128)S(1)}, u32[]{:S(2)}, u32[]{:S(2)}) collective-permute-start(f32[4,6,1,128]{3,2,1,0:T(1,128)S(1)} %get-tuple-element.121), channel_id=1, source_target_pairs={{1,0},{2,1},{3,2},{5,4},{6,5},{7,6},{9,8},{10,9},{11,10},{13,12},{... | collective-permute-start | bytes 36872 | tf_op jit(solution)/shard_map/ppermute | solution.py:23
  84.7 9.4 %collective-permute-start.6 = (f32[4,6,1,128]{3,2,1,0:T(1,128)S(1)}, f32[4,6,1,128]{3,2,1,0:T(1,128)S(1)}, u32[]{:S(2)}, u32[]{:S(2)}) collective-permute-start(f32[4,6,1,128]{3,2,1,0:T(1,128)S(1)} %get-tuple-element.120), channel_id=1, source_target_pairs={{0,1},{1,2},{2,3},{4,5},{5,6},{6,7},{8,9},{9,10},{10,11},{12,13},{... | collective-permute-start | bytes 36872 | tf_op jit(solution)/shard_map/ppermute | solution.py:20
  100.5 8.0 %collective-permute-start.11 = (f32[4,6,1,128]{3,2,1,0:T(1,128)S(1)}, f32[4,6,1,128]{3,2,1,0:T(1,128)S(1)}, u32[]{:S(2)}, u32[]{:S(2)}) collective-permute-start(f32[4,6,1,128]{3,2,1,0:T(1,128)S(1)} %get-tuple-element.119), channel_id=1, source_target_pairs={{1,0},{2,1},{3,2},{5,4},{6,5},{7,6},{9,8},{10,9},{11,10},{13,12},{... | collective-permute-start | bytes 36872 | tf_op jit(solution)/shard_map/ppermute | solution.py:23
  136.1 15.5 %collective-permute-start.19 = (f32[4,6,1,128]{3,2,1,0:T(1,128)S(1)}, f32[4,6,1,128]{3,2,1,0:T(1,128)S(1)}, u32[]{:S(2)}, u32[]{:S(2)}) collective-permute-start(f32[4,6,1,128]{3,2,1,0:T(1,128)S(1)} %get-tuple-element.115), channel_id=1, source_target_pairs={{1,0},{2,1},{3,2},{5,4},{6,5},{7,6},{9,8},{10,9},{11,10},{13,12},{... | collective-permute-start | bytes 36872 | tf_op jit(solution)/shard_map/ppermute | solution.py:23
  138.0 13.6 %collective-permute-start.18 = (f32[4,6,1,128]{3,2,1,0:T(1,128)S(1)}, f32[4,6,1,128]{3,2,1,0:T(1,128)S(1)}, u32[]{:S(2)}, u32[]{:S(2)}) collective-permute-start(f32[4,6,1,128]{3,2,1,0:T(1,128)S(1)} %get-tuple-element.114), channel_id=1, source_target_pairs={{0,1},{1,2},{2,3},{4,5},{5,6},{6,7},{8,9},{9,10},{10,11},{12,13},{... | collective-permute-start | bytes 36872 | tf_op jit(solution)/shard_map/ppermute | solution.py:20
  144.7 32.1 %collective-permute-start.32 = (f32[4,1,32,128]{3,2,1,0:T(8,128)}, f32[4,1,32,128]{3,2,1,0:T(8,128)S(1)}, u32[]{:S(2)}, u32[]{:S(2)}) collective-permute-start(f32[4,1,32,128]{3,2,1,0:T(8,128)} %get-tuple-element.137), channel_id=1, source_target_pairs={{0,4},{4,8},{8,12},{12,16},{16,20},{20,24},{24,28},{28,32},{32,36}... | collective-permute-start | bytes 196616 | tf_op jit(solution)/shard_map/ppermute | solution.py:20
  150.2 43.6 %collective-permute-start.33 = (f32[4,1,32,128]{3,2,1,0:T(8,128)}, f32[4,1,32,128]{3,2,1,0:T(8,128)}, u32[]{:S(2)}, u32[]{:S(2)}) collective-permute-start(f32[4,1,32,128]{3,2,1,0:T(8,128)} %get-tuple-element.136), channel_id=1, source_target_pairs={{4,0},{8,4},{12,8},{16,12},{20,16},{24,20},{28,24},{32,28},{36,32}... | collective-permute-start | bytes 196616 | tf_op jit(solution)/shard_map/ppermute | solution.py:23
  160.5 9.8 %collective-permute-start.23 = (f32[4,6,1,128]{3,2,1,0:T(1,128)}, f32[4,6,1,128]{3,2,1,0:T(1,128)}, u32[]{:S(2)}, u32[]{:S(2)}) collective-permute-start(f32[4,6,1,128]{3,2,1,0:T(1,128)} %get-tuple-element.113), channel_id=1, source_target_pairs={{1,0},{2,1},{3,2},{5,4},{6,5},{7,6},{9,8},{10,9},{11,10},{13,12},{... | collective-permute-start | bytes 36872 | tf_op jit(solution)/shard_map/ppermute | solution.py:23
  177.7 8.0 %collective-permute-start.27 = (f32[4,6,1,128]{3,2,1,0:T(1,128)S(1)}, f32[4,6,1,128]{3,2,1,0:T(1,128)S(1)}, u32[]{:S(2)}, u32[]{:S(2)}) collective-permute-start(f32[4,6,1,128]{3,2,1,0:T(1,128)S(1)} %get-tuple-element.111), channel_id=1, source_target_pairs={{1,0},{2,1},{3,2},{5,4},{6,5},{7,6},{9,8},{10,9},{11,10},{13,12},{... | collective-permute-start | bytes 36872 | tf_op jit(solution)/shard_map/ppermute | solution.py:23
  194.7 16.0 %collective-permute-start.31 = (f32[4,6,1,128]{3,2,1,0:T(1,128)S(1)}, f32[4,6,1,128]{3,2,1,0:T(1,128)S(1)}, u32[]{:S(2)}, u32[]{:S(2)}) collective-permute-start(f32[4,6,1,128]{3,2,1,0:T(1,128)S(1)} %get-tuple-element.109), channel_id=1, source_target_pairs={{1,0},{2,1},{3,2},{5,4},{6,5},{7,6},{9,8},{10,9},{11,10},{13,12},{... | collective-permute-start | bytes 36872 | tf_op jit(solution)/shard_map/ppermute | solution.py:23
  196.6 14.0 %collective-permute-start.30 = (f32[4,6,1,128]{3,2,1,0:T(1,128)S(1)}, f32[4,6,1,128]{3,2,1,0:T(1,128)S(1)}, u32[]{:S(2)}, u32[]{:S(2)}) collective-permute-start(f32[4,6,1,128]{3,2,1,0:T(1,128)S(1)} %get-tuple-element.108), channel_id=1, source_target_pairs={{0,1},{1,2},{2,3},{4,5},{5,6},{6,7},{8,9},{9,10},{10,11},{12,13},{... | collective-permute-start | bytes 36872 | tf_op jit(solution)/shard_map/ppermute | solution.py:20
  202.7 53.4 %collective-permute-start.35 = (f32[4,6,1,128]{3,2,1,0:T(1,128)S(1)}, f32[4,6,1,128]{3,2,1,0:T(1,128)S(1)}, u32[]{:S(2)}, u32[]{:S(2)}) collective-permute-start(f32[4,6,1,128]{3,2,1,0:T(1,128)S(1)} %get-tuple-element.107), channel_id=1, source_target_pairs={{1,0},{2,1},{3,2},{5,4},{6,5},{7,6},{9,8},{10,9},{11,10},{13,12},{... | collective-permute-start | bytes 36872 | tf_op jit(solution)/shard_map/ppermute | solution.py:23
  204.6 51.5 %collective-permute-start.34 = (f32[4,6,1,128]{3,2,1,0:T(1,128)S(1)}, f32[4,6,1,128]{3,2,1,0:T(1,128)S(1)}, u32[]{:S(2)}, u32[]{:S(2)}) collective-permute-start(f32[4,6,1,128]{3,2,1,0:T(1,128)S(1)} %get-tuple-element.106), channel_id=1, source_target_pairs={{0,1},{1,2},{2,3},{4,5},{5,6},{6,7},{8,9},{9,10},{10,11},{12,13},{... | collective-permute-start | bytes 36872 | tf_op jit(solution)/shard_map/ppermute | solution.py:20
  262.5 8.0 %collective-permute-start.39 = (f32[4,6,1,128]{3,2,1,0:T(1,128)S(1)}, f32[4,6,1,128]{3,2,1,0:T(1,128)S(1)}, u32[]{:S(2)}, u32[]{:S(2)}) collective-permute-start(f32[4,6,1,128]{3,2,1,0:T(1,128)S(1)} %get-tuple-element.105), channel_id=1, source_target_pairs={{1,0},{2,1},{3,2},{5,4},{6,5},{7,6},{9,8},{10,9},{11,10},{13,12},{... | collective-permute-start | bytes 36872 | tf_op jit(solution)/shard_map/ppermute | solution.py:23
  296.5 8.0 %collective-permute-start.47 = (f32[4,6,1,128]{3,2,1,0:T(1,128)S(1)}, f32[4,6,1,128]{3,2,1,0:T(1,128)S(1)}, u32[]{:S(2)}, u32[]{:S(2)}) collective-permute-start(f32[4,6,1,128]{3,2,1,0:T(1,128)S(1)} %get-tuple-element.101), channel_id=1, source_target_pairs={{1,0},{2,1},{3,2},{5,4},{6,5},{7,6},{9,8},{10,9},{11,10},{13,12},{... | collective-permute-start | bytes 36872 | tf_op jit(solution)/shard_map/ppermute | solution.py:23
  314.3 8.0 %collective-permute-start.51 = (f32[4,6,1,128]{3,2,1,0:T(1,128)S(1)}, f32[4,6,1,128]{3,2,1,0:T(1,128)S(1)}, u32[]{:S(2)}, u32[]{:S(2)}) collective-permute-start(f32[4,6,1,128]{3,2,1,0:T(1,128)S(1)} %get-tuple-element.99), channel_id=1, source_target_pairs={{1,0},{2,1},{3,2},{5,4},{6,5},{7,6},{9,8},{10,9},{11,10},{13,12},{... | collective-permute-start | bytes 36872 | tf_op jit(solution)/shard_map/ppermute | solution.py:23
  367.1 8.8 %collective-permute-start.63 = (f32[8,6,1,128]{3,2,1,0:T(1,128)S(1)}, f32[8,6,1,128]{3,2,1,0:T(1,128)S(1)}, u32[]{:S(2)}, u32[]{:S(2)}) collective-permute-start(f32[8,6,1,128]{3,2,1,0:T(1,128)S(1)} %get-tuple-element.83), channel_id=1, source_target_pairs={{1,0},{2,1},{3,2},{5,4},{6,5},{7,6},{9,8},{10,9},{11,10},{13,12},{... | collective-permute-start | bytes 73736 | tf_op jit(solution)/shard_map/ppermute | solution.py:23
  (62 other events, 679.1 us)
Sparse Core Ops, SparseCore 0:
  377.9 99.7 all-reduce.20
